TPU v7x, 512 devices: a whole 4x8x8 slice. The times are simulated.
512 devices in a mesh: tm: 16 (over x_lo, y), space: 32 (over x_hi, z, core).
Axes of the slice: x: 4 (x_hi: 2, x_lo: 2; x = x_hi * 2 + x_lo), y: 8, z: 8, core: 2. Of those that a mesh axis runs over, the one named last changes fastest.
Arguments:
- adjoint_start: float32 [32, 5, 192, 2048], P('tm', None, 'space'), may hold values from -6 to 6
- source: float32 [32, 5, 192, 2048], P('tm', None, 'space'), may hold values from -6 to 6
- inv_diagonal: bfloat16 [5, 5, 192, 2048], P(None, None, 'space'), may hold values from -0.081 to 0.35
- east_block: bfloat16 [5, 5, 192, 2048], P(None, None, 'space'), may hold values from -1.796875 to 1.796875
- west_block: bfloat16 [5, 5, 192, 2048], P(None, None, 'space'), may hold values from -1.796875 to 1.796875
- pair_block: bfloat16 [5, 5, 192, 2048], P(None, None, 'space'), may hold values from -1.796875 to 1.796875
- time_scale: float32 [192, 2048], P('space'), may hold values from 0.02 to 0.2
- partner: int32 [192, 2048], P('space'), may hold values from 0 to 5, as said below
Outputs:
- adjoint: float32 [32, 5, 192, 2048], P('tm', None, 'space')
Inputs may be any that keep to these rules, and one draw needn't show every extreme that they name: In each column r and each block of 6 cells along the first dimension starting at a multiple of 6, partner pairs the block's cells: the partner of a cell's partner is the cell itself, and no cell is its own partner.
All inputs are finite; a program needn't handle non-finite values.
Results may differ from a plain program's by a relative error of at most 0.0003.
Values sent between devices are 32-bit elements; how exact they have to be, the bound alone decides.
A program may use at most 64 MiB of HBM per device.

v0:
```python
import math

import jax
import jax.numpy as jnp
from jax import lax
from jax.sharding import PartitionSpec as P

ITERS = 2


def from_behind(value, axis, steps):
    count = lax.axis_size(axis)
    first, last = (max(0, -steps), min(count, count - steps))
    return lax.ppermute(value, axis, [(source, source + steps) for source in range(first, last)])


def apply_transposed(matrix, vector):
    total = matrix[0][None].astype(jnp.float32) * vector[:, 0:1]
    for column in range(1, 5):
        total = total + matrix[column][None].astype(jnp.float32) * vector[:, column : column + 1]
    return total


def spectral_matrix(rows_global, cols_global, count):
    gap = jnp.mod(rows_global[:, None] - cols_global[None, :], count)
    angle = math.pi * gap.astype(jnp.float32) / count
    parity = (2 * jnp.mod(gap, 2) - 1).astype(jnp.float32)
    safe = jnp.where(gap == 0, 1.0, jnp.sin(angle))
    value = 0.5 * parity * jnp.cos(angle) / safe
    dead = jnp.logical_or(gap == 0, 2 * gap == count)
    return jnp.where(dead, 0.0, value)


def pick_partner(pair_term, partner):
    cells = pair_term.shape[2]
    chosen = jnp.zeros(pair_term.shape, jnp.float32)
    for source_cell in range(cells):
        hit = (partner == source_cell)[None, None]
        chosen = chosen + jnp.where(hit, pair_term[:, :, source_cell : source_cell + 1], 0.0)
    return chosen


def spatial_terms(adjoint, east_block, west_block, pair_block, partner):
    east_term = apply_transposed(east_block, adjoint)
    west_term = apply_transposed(west_block, adjoint)
    pair_term = apply_transposed(pair_block, adjoint)
    from_below = from_behind(east_term[:, :, -1:], "space", 1)
    from_above = from_behind(west_term[:, :, :1], "space", -1)
    east_in = jnp.concatenate([from_below, east_term[:, :, :-1]], axis=2)
    west_in = jnp.concatenate([west_term[:, :, 1:], from_above], axis=2)
    pair_in = pick_partner(pair_term, partner)
    return east_in + west_in + pair_in


def local(
    adjoint_start, source, inv_diagonal, east_block, west_block, pair_block, time_scale, partner
):
    adjoint = adjoint_start
    local_count = adjoint.shape[0]
    count = local_count * lax.axis_size("tm")
    own_rows = lax.axis_index("tm") * local_count + jnp.arange(local_count, dtype=jnp.int32)
    for iteration in range(ITERS):
        piece = lax.all_gather(adjoint, "tm", axis=0, tiled=True)
        cols = jnp.arange(piece.shape[0], dtype=jnp.int32)
        coupling = spectral_matrix(own_rows, cols, count)
        band_sum = jnp.einsum("nm,mvxr->nvxr", coupling, piece, precision=lax.Precision.HIGHEST)
        offdiag = spatial_terms(adjoint, east_block, west_block, pair_block, partner)
        time_term = time_scale[None, None] * band_sum
        adjoint = apply_transposed(inv_diagonal, source - offdiag - time_term)
    return adjoint


def solution(mesh):
    return jax.shard_map(
        local,
        mesh=mesh,
        in_specs=(
            P("tm", None, "space", None),
            P("tm", None, "space", None),
            P(None, None, "space", None),
            P(None, None, "space", None),
            P(None, None, "space", None),
            P(None, None, "space", None),
            P("space", None),
            P("space", None),
        ),
        out_specs=P("tm", None, "space", None),
        check_vma=False,
    )
```

profile of v0, /device:TPU:1, one launch (start us, length us, event | category | flops | bytes accessed | tf_op | source)
XLA Modules:
  0.0 300.2 jit_solution(8515962622280322630)
XLA Ops:
  6.5 2.2 copy.9
  8.8 1.1 slice_bitcast_fusion.19
  9.9 1.4 bitcast_convert_fusion.18
  12.0 5.4 %collective-permute-start = (f32[2,5,1,2048]{3,0,2,1:T(2,128)S(1)}, f32[2,5,1,2048]{3,0,2,1:T(2,128)}, u32[]{:S(2)}, u32[]{:S(2)}) collective-permute-start(f32[2,5,1,2048]{3,0,2,1:T(2,128)S(1)} %slice.280), channel_id=1, source_target_pairs={{0,1},{1,2},{2,3},{3,4},{4,5},{5,6},{6,7},{7,8},{8,9},{9,10},{10,1... | collective-permute-start | bytes 245768 | tf_op jit(solution)/shard_map/ppermute | solution.py:14
  17.4 1.8 bitcast_convert_fusion.8
  19.2 2.3 multiply_add_fusion.5
  21.5 5.3 %collective-permute-start.1 = (f32[2,5,1,2048]{3,0,2,1:T(2,128)S(1)}, f32[2,5,1,2048]{3,0,2,1:T(2,128)}, u32[]{:S(2)}, u32[]{:S(2)}) collective-permute-start(f32[2,5,1,2048]{3,0,2,1:T(2,128)S(1)} %slice.283), channel_id=1, source_target_pairs={{1,0},{2,1},{3,2},{4,3},{5,4},{6,5},{7,6},{8,7},{9,8},{10,9},{11,1... | collective-permute-start | bytes 245768 | tf_op jit(solution)/shard_map/ppermute | solution.py:14
  26.8 0.8 slice.281
  27.6 0.8 slice.282
  28.4 0.7 broadcast_compare_fusion.5
  29.1 1.9 slice_bitcast_fusion.31
  31.0 2.4 bitcast_convert_fusion.19
  33.9 105.4 %all-gather.3.cloned.1.call-done = f32[32,5,6,2048]{3,2,1,0:T(8,128)} async-done(((f32[2,5,6,2048]{3,2,1,0:T(8,128)}), f32[32,5,6,2048]{3,2,1,0:T(8,128)}) %all-gather.3.cloned.1.call-update) | async-done | bytes 7864336 | tf_op jit(solution)/shard_map/all_gather | solution.py:63
  139.3 13.9 %fusion.12 = f32[2,5,6,2048]{3,0,2,1:T(2,128)S(1)} fusion(f32[2,5,6,2048]{3,0,2,1:T(2,128)} %param.9, f32[2,5,5,2048]{3,0,2,1:T(2,128)} %slice.281, f32[2,5,1,2048]{3,0,2,1:T(2,128)} %collective-permute-done, f32[2,5,1,2048]{3,0,2,1:T(2,128)} %collective-permute-done.1, f32[2,5,5,2048]{3,0,2,1:T(2,128)} %slice.282, pred[6,2048]{1,0:T(8,128)(4,1)} %get-tuple-element.65, ...), kind=kOutput, calls=%fused_computation.11 | convolution fusion | flops 49400128 | bytes 10444808 | tf_op jit(solution)/shard_map/nm,mvxr->nvxr/dot_general | solution.py:66
  153.7 1.0 multiply_add_fusion.1
  154.8 1.2 slice_bitcast_fusion.4
  156.4 2.0 multiply_add_fusion.4
  158.5 3.8 %collective-permute-start.2 = (f32[2,5,1,2048]{3,0,2,1:T(2,128)S(1)}, f32[2,5,1,2048]{3,0,2,1:T(2,128)S(1)}, u32[]{:S(2)}, u32[]{:S(2)}) collective-permute-start(f32[2,5,1,2048]{3,0,2,1:T(2,128)S(1)} %slice.300), channel_id=1, source_target_pairs={{0,1},{1,2},{2,3},{3,4},{4,5},{5,6},{6,7},{7,8},{8,9},{9,10},{10,1... | collective-permute-start | bytes 245768 | tf_op jit(solution)/shard_map/ppermute | solution.py:14
  162.3 1.6 multiply_add_fusion.2
  164.0 2.2 collective-permute-start.3
  166.4 3.9 %collective-permute-done.3 = f32[2,5,1,2048]{3,0,2,1:T(2,128)S(1)} collective-permute-done((f32[2,5,1,2048]{3,0,2,1:T(2,128)S(1)}, f32[2,5,1,2048]{3,0,2,1:T(2,128)S(1)}, u32[]{:S(2)}, u32[]{:S(2)}) %collective-permute-start.3) | collective-permute-done | bytes 81952 | tf_op jit(solution)/shard_map/ppermute | solution.py:14
  170.3 107.2 %all-gather.5.cloned.1.call-done = f32[32,5,6,2048]{3,2,1,0:T(8,128)} async-done(((f32[2,5,6,2048]{3,2,1,0:T(8,128)}), f32[32,5,6,2048]{3,2,1,0:T(8,128)}) %all-gather.5.cloned.1.call-update) | async-done | bytes 7864336 | tf_op jit(solution)/shard_map/all_gather | solution.py:63
  277.5 13.9 %fusion.15 = f32[2,5,6,2048]{3,0,2,1:T(2,128)S(1)} fusion(f32[2,5,6,2048]{3,0,2,1:T(2,128)} %param.9, f32[2,5,5,2048]{3,0,2,1:T(2,128)S(1)} %slice.301, f32[2,5,1,2048]{3,0,2,1:T(2,128)S(1)} %collective-permute-done.2, f32[2,5,1,2048]{3,0,2,1:T(2,128)S(1)} %collective-permute-done.3, f32[2,5,5,2048]{3,0,2,1:T(2,128)S(1)} %slice.302, ...), kind=kOutput, calls=%fused_computation.15 | convolution fusion | flops 49400128 | bytes 10444808 | tf_op jit(solution)/shard_map/nm,mvxr->nvxr/dot_general | solution.py:66
  292.2 1.2 copy.27
  (76 shorter events, 2.8 us)
Async XLA Ops:
  6.5 21.9 %copy-start.15 = (s32[6,2048]{1,0:T(8,128)S(1)}, s32[6,2048]{1,0:T(8,128)}, u32[]{:S(2)}) copy-start(s32[6,2048]{1,0:T(8,128)} %param.15) | copy-start | bytes 147460
  6.5 132.8 %all-gather.3.cloned.1.call-start = ((), (), s32[]{:S(2)}) async-start(), calls=%async_computation | async-start | bytes 11141120 | tf_op jit(solution)/shard_map/all_gather | solution.py:63
  8.8 268.7 %all-gather.5.cloned.1.call-start = ((), (), s32[]{:S(2)}) async-start(), calls=%async_computation.1 | async-start | bytes 11141120 | tf_op jit(solution)/shard_map/all_gather | solution.py:63
  11.3 7.9 %copy-start.2 = (f32[5,6,2048]{2,1,0:T(8,128)}, f32[5,6,2048]{2,1,0:T(8,128)S(1)}, u32[]{:S(2)}) copy-start(f32[5,6,2048]{2,1,0:T(8,128)S(1)} %get-tuple-element.22) | copy-start | bytes 737284
  11.3 7.9 %copy-start.3 = (f32[5,6,2048]{2,1,0:T(8,128)}, f32[5,6,2048]{2,1,0:T(8,128)S(1)}, u32[]{:S(2)}) copy-start(f32[5,6,2048]{2,1,0:T(8,128)S(1)} %get-tuple-element.23) | copy-start | bytes 737284
  12.0 21.9 %collective-permute-start = (f32[2,5,1,2048]{3,0,2,1:T(2,128)S(1)}, f32[2,5,1,2048]{3,0,2,1:T(2,128)}, u32[]{:S(2)}, u32[]{:S(2)}) collective-permute-start(f32[2,5,1,2048]{3,0,2,1:T(2,128)S(1)} %slice.280), channel_id=1, source_target_pairs={{0,1},{1,2},{2,3},{3,4},{4,5},{5,6},{6,7},{7,8},{8,9},{9,10},{10,1... | collective-permute-start | bytes 245768 | tf_op jit(solution)/shard_map/ppermute | solution.py:14
  21.5 12.4 %collective-permute-start.1 = (f32[2,5,1,2048]{3,0,2,1:T(2,128)S(1)}, f32[2,5,1,2048]{3,0,2,1:T(2,128)}, u32[]{:S(2)}, u32[]{:S(2)}) collective-permute-start(f32[2,5,1,2048]{3,0,2,1:T(2,128)S(1)} %slice.283), channel_id=1, source_target_pairs={{1,0},{2,1},{3,2},{4,3},{5,4},{6,5},{7,6},{8,7},{9,8},{10,9},{11,1... | collective-permute-start | bytes 245768 | tf_op jit(solution)/shard_map/ppermute | solution.py:14
  139.3 14.4 %copy-start.5 = (f32[5,6,2048]{2,1,0:T(8,128)S(1)}, f32[5,6,2048]{2,1,0:T(8,128)}, u32[]{:S(2)}) copy-start(f32[5,6,2048]{2,1,0:T(8,128)} %get-tuple-element.5) | copy-start | bytes 737284
  139.3 14.4 %copy-start.7 = (f32[5,6,2048]{2,1,0:T(8,128)S(1)}, f32[5,6,2048]{2,1,0:T(8,128)}, u32[]{:S(2)}) copy-start(f32[5,6,2048]{2,1,0:T(8,128)} %get-tuple-element.6) | copy-start | bytes 737284
  139.3 14.4 %copy-start.9 = (f32[5,6,2048]{2,1,0:T(8,128)S(1)}, f32[5,6,2048]{2,1,0:T(8,128)}, u32[]{:S(2)}) copy-start(f32[5,6,2048]{2,1,0:T(8,128)} %get-tuple-element.7) | copy-start | bytes 737284
  139.3 14.4 %copy-start.11 = (f32[5,6,2048]{2,1,0:T(8,128)S(1)}, f32[5,6,2048]{2,1,0:T(8,128)}, u32[]{:S(2)}) copy-start(f32[5,6,2048]{2,1,0:T(8,128)} %get-tuple-element.8) | copy-start | bytes 737284
  139.3 14.4 %copy-start.13 = (f32[5,6,2048]{2,1,0:T(8,128)S(1)}, f32[5,6,2048]{2,1,0:T(8,128)}, u32[]{:S(2)}) copy-start(f32[5,6,2048]{2,1,0:T(8,128)} %get-tuple-element.9) | copy-start | bytes 737284
  153.2 124.2 %copy-start.16 = (pred[6,2048]{1,0:T(8,128)(4,1)S(1)}, pred[6,2048]{1,0:T(8,128)(4,1)}, u32[]{:S(2)}) copy-start(pred[6,2048]{1,0:T(8,128)(4,1)} %get-tuple-element.63) | copy-start | bytes 36868
  153.2 124.2 %copy-start.17 = (pred[6,2048]{1,0:T(8,128)(4,1)S(1)}, pred[6,2048]{1,0:T(8,128)(4,1)}, u32[]{:S(2)}) copy-start(pred[6,2048]{1,0:T(8,128)(4,1)} %get-tuple-element.64) | copy-start | bytes 36868
  153.3 124.2 %copy-start.18 = (pred[6,2048]{1,0:T(8,128)(4,1)S(1)}, pred[6,2048]{1,0:T(8,128)(4,1)}, u32[]{:S(2)}) copy-start(pred[6,2048]{1,0:T(8,128)(4,1)} %get-tuple-element.65) | copy-start | bytes 36868
  153.3 124.2 %copy-start.19 = (pred[6,2048]{1,0:T(8,128)(4,1)S(1)}, pred[6,2048]{1,0:T(8,128)(4,1)}, u32[]{:S(2)}) copy-start(pred[6,2048]{1,0:T(8,128)(4,1)} %get-tuple-element.66) | copy-start | bytes 36868
  153.3 124.2 %copy-start.20 = (s32[2]{0:T(128)S(1)}, s32[2]{0:T(128)}, u32[]{:S(2)}) copy-start(s32[2]{0:T(128)} %iota_add_fusion) | copy-start | bytes 28
  158.5 7.9 %collective-permute-start.2 = (f32[2,5,1,2048]{3,0,2,1:T(2,128)S(1)}, f32[2,5,1,2048]{3,0,2,1:T(2,128)S(1)}, u32[]{:S(2)}, u32[]{:S(2)}) collective-permute-start(f32[2,5,1,2048]{3,0,2,1:T(2,128)S(1)} %slice.300), channel_id=1, source_target_pairs={{0,1},{1,2},{2,3},{3,4},{4,5},{5,6},{6,7},{7,8},{8,9},{9,10},{10,1... | collective-permute-start | bytes 245768 | tf_op jit(solution)/shard_map/ppermute | solution.py:14
  163.9 127.9 %copy-start.6 = (f32[5,6,2048]{2,1,0:T(8,128)S(1)}, f32[5,6,2048]{2,1,0:T(8,128)}, u32[]{:S(2)}) copy-start(f32[5,6,2048]{2,1,0:T(8,128)} %get-tuple-element.5) | copy-start | bytes 737284
  163.9 127.9 %copy-start.8 = (f32[5,6,2048]{2,1,0:T(8,128)S(1)}, f32[5,6,2048]{2,1,0:T(8,128)}, u32[]{:S(2)}) copy-start(f32[5,6,2048]{2,1,0:T(8,128)} %get-tuple-element.6) | copy-start | bytes 737284
  164.0 127.9 %copy-start.10 = (f32[5,6,2048]{2,1,0:T(8,128)S(1)}, f32[5,6,2048]{2,1,0:T(8,128)}, u32[]{:S(2)}) copy-start(f32[5,6,2048]{2,1,0:T(8,128)} %get-tuple-element.7) | copy-start | bytes 737284
  164.0 127.9 %copy-start.12 = (f32[5,6,2048]{2,1,0:T(8,128)S(1)}, f32[5,6,2048]{2,1,0:T(8,128)}, u32[]{:S(2)}) copy-start(f32[5,6,2048]{2,1,0:T(8,128)} %get-tuple-element.8) | copy-start | bytes 737284
  164.0 127.9 %copy-start.14 = (f32[5,6,2048]{2,1,0:T(8,128)S(1)}, f32[5,6,2048]{2,1,0:T(8,128)}, u32[]{:S(2)}) copy-start(f32[5,6,2048]{2,1,0:T(8,128)} %get-tuple-element.9) | copy-start | bytes 737284
  164.0 6.3 %collective-permute-start.3 = (f32[2,5,1,2048]{3,0,2,1:T(2,128)S(1)}, f32[2,5,1,2048]{3,0,2,1:T(2,128)S(1)}, u32[]{:S(2)}, u32[]{:S(2)}) collective-permute-start(f32[2,5,1,2048]{3,0,2,1:T(2,128)S(1)} %slice.303), channel_id=1, source_target_pairs={{1,0},{2,1},{3,2},{4,3},{5,4},{6,5},{7,6},{8,7},{9,8},{10,9},{11,1... | collective-permute-start | bytes 245768 | tf_op jit(solution)/shard_map/ppermute | solution.py:14
  (3 other events, 14.8 us)
Sparse Core Ops, SparseCore 0:
  9.4 129.8 all-gather.2
  154.9 122.4 all-gather.4
where the time goes:
time: 301 us; the launch traced here: 300 us
  waiting for transfers between devices  217 us (72%)
  matrix products  27.8 us (9%)
  starting transfers between devices  16.8 us (6%)
  other arithmetic  14.6 us (5%)
  between operations  13.9 us (5%)
  local copies, waits for them, and re-layouts  10.5 us (3%)
    all_gather x2, waiting for transfers between devices, local(): piece = lax.all_gather(adjoint, 'tm', axis=0, tiled=True)  213 us
    dot_general x2, matrix products, local(): jnp.einsum('nm,mvxr->nvxr', coupling, piece, precision=lax.Precision.HIGH...  27.8 us
    ppermute x4, starting transfers between devices, from_behind(): lax.ppermute(value, axis, [(source, source + steps) for source in range(f...  16.7 us
    add x6, other arithmetic, apply_transposed(): total + matrix[column][None].astype(jnp.float32) * vector[:, column:colum...  7.84 us
  transfers between devices with their start and end apart: 6, of which 3 were waited for; matrix products, arithmetic and copies ran while one was open for 7% of the time, Pallas kernels for 0%

commit v1 on v0

v1 whole, which is shorter than its diff:
```python
import math

import jax
import jax.numpy as jnp
from jax import lax
from jax.experimental import pallas as pl
from jax.experimental.pallas import tpu as pltpu
from jax.sharding import PartitionSpec as P

MESH = pl.DeviceIdType.MESH
TM = 16
RING = 8
SPACE = 32
INST = 32
OWN = INST // TM
VARS = 5
CX = 6
LANES = 128
ROWS = 8
BLOCK = 4

PEERS = [
    (across, along)
    for along in (4, 3, 5, 2, 6, 1, 7, 0)
    for across in (1, 0)
    if (across, along) != (0, 0)
]


def time_weights():
    return [
        0.0 if d in (0, INST // 2) else 0.5 * (-1) ** (d + 1) / math.tan(math.pi * d / INST)
        for d in range(INST)
    ]


def negacyclic(weights, value):
    count = len(weights)
    back = -value
    wide = jnp.concatenate([back, value, back], axis=0)
    half = count // 2
    total = weights[half] * wide[count - half : 2 * count - half]
    for d in range(1, half):
        total = total + weights[d] * (wide[count - d : 2 * count - d] - wide[count + d : 2 * count + d])
    return total


def cyclic(weights, value):
    count = len(weights)
    if count == 8:
        wide = jnp.concatenate([value, value, value], axis=0)
        total = None
        for d in range(1, count // 2):
            term = weights[d] * (wide[count - d : 2 * count - d] - wide[count + d : 2 * count + d])
            total = term if total is None else total + term
        return total
    half = count // 2
    low, high = value[:half], value[half:]
    plus = cyclic([0.5 * (weights[d] + weights[d + half]) for d in range(half)], low + high)
    minus = negacyclic([0.5 * (weights[d] - weights[d + half]) for d in range(half)], low - high)
    return jnp.concatenate([plus + minus, plus - minus], axis=0)


def kernel(
    start_hbm,
    source_hbm,
    inv_hbm,
    east_hbm,
    west_hbm,
    pair_hbm,
    scale_hbm,
    partner_hbm,
    out_hbm,
    first,
    source,
    second,
    offdiag,
    result,
    packed,
    blocks,
    scale,
    partner,
    east_out,
    west_out,
    east_in,
    west_in,
    local_sem,
    send_sem,
    recv_sem,
    halo_send,
    halo_recv,
    back_send,
    back_recv,
):
    tm, space = lax.axis_index("tm"), lax.axis_index("space")
    across, along = tm // RING, lax.rem(tm, RING)
    INV, EAST, WEST, PAIR = range(4)
    flat = lambda ref: ref.reshape(INST * VARS * ROWS, LANES)
    columns = lambda who: pl.ds(pl.multiple_of(who * LANES, LANES), LANES)
    cells = pl.ds(0, CX)

    own = []
    for slot, block_hbm in enumerate((inv_hbm, east_hbm, west_hbm, pair_hbm)):
        own.append(
            pltpu.make_async_copy(block_hbm.at[:, :, :, columns(tm)], packed.at[slot], local_sem.at[slot])
        )
    own.append(pltpu.make_async_copy(scale_hbm.at[:, columns(tm)], scale.at[cells], local_sem.at[4]))
    own.append(pltpu.make_async_copy(partner_hbm.at[:, columns(tm)], partner.at[cells], local_sem.at[5]))
    for slot, (field_hbm, field) in enumerate(((start_hbm, first), (source_hbm, source))):
        own.append(
            pltpu.make_async_copy(
                field_hbm.at[:, :, :, columns(tm)],
                field.at[pl.ds(tm * OWN, OWN), :, cells, :],
                local_sem.at[6 + slot],
            )
        )
    for copy in own:
        copy.start()

    barrier = pltpu.get_barrier_semaphore()
    peers = [
        lax.rem(across + da, 2) * RING + lax.rem(along + dy, RING) for da, dy in PEERS
    ]
    for peer in peers:
        pl.semaphore_signal(barrier, inc=1, device_id=(peer, space), device_id_type=MESH)
    has_next, has_previous = space < SPACE - 1, space > 0

    @pl.when(has_next)
    def _():
        pl.semaphore_signal(barrier, inc=1, device_id=(tm, space + 1), device_id_type=MESH)

    @pl.when(has_previous)
    def _():
        pl.semaphore_signal(barrier, inc=1, device_id=(tm, space - 1), device_id_type=MESH)

    pl.semaphore_wait(barrier, len(peers) + has_next.astype(jnp.int32) + has_previous.astype(jnp.int32))

    gathers = []
    for slot, (field_hbm, field) in enumerate(((start_hbm, first), (source_hbm, source))):
        copies = []
        for step, peer in enumerate(peers):
            copy = pltpu.make_async_remote_copy(
                src_ref=field_hbm.at[:, :, :, columns(peer)],
                dst_ref=field.at[pl.ds(tm * OWN, OWN), :, cells, :],
                send_sem=send_sem.at[slot, step],
                recv_sem=recv_sem.at[slot, step],
                device_id=(peer, space),
                device_id_type=MESH,
            )
            copy.start()
            copies.append(copy)
        gathers.append(copies)

    for copy in own[:6]:
        copy.wait()
    for slot in range(4):
        for a in range(VARS):
            blocks[slot, a, :, cells, :] = packed[slot, a].astype(jnp.float32)
    row = lax.broadcasted_iota(jnp.int32, (1, ROWS, LANES), 1)
    partner[...] = jnp.where(row[0] < CX, partner[...], 0)

    def halo_copies(turn):
        east = pltpu.make_async_remote_copy(
            src_ref=east_out.at[turn],
            dst_ref=east_in.at[turn],
            send_sem=halo_send.at[turn, 0],
            recv_sem=halo_recv.at[turn, 0],
            device_id=(tm, space + 1),
            device_id_type=MESH,
        )
        west = pltpu.make_async_remote_copy(
            src_ref=west_out.at[turn],
            dst_ref=west_in.at[turn],
            send_sem=halo_send.at[turn, 1],
            recv_sem=halo_recv.at[turn, 1],
            device_id=(tm, space - 1),
            device_id_type=MESH,
        )
        return east, west

    def send_halo(turn, field):
        view = flat(field)
        for block, cell, out in ((EAST, CX - 1, east_out), (WEST, 0, west_out)):
            edge = [view[pl.ds(a * ROWS + cell, INST, stride=VARS * ROWS), :] for a in range(VARS)]
            for i in range(VARS):
                total = blocks[block, 0, i, pl.ds(cell, 1), :] * edge[0]
                for a in range(1, VARS):
                    total = total + blocks[block, a, i, pl.ds(cell, 1), :] * edge[a]
                out[turn, i] = total
        east, west = halo_copies(turn)

        @pl.when(has_next)
        def _():
            east.start()

        @pl.when(has_previous)
        def _():
            west.start()

    def take_halo(turn):
        east, west = halo_copies(turn)
        view = flat(offdiag)

        @pl.when(has_previous)
        def _():
            east.wait_recv()
            for i in range(VARS):
                at = pl.ds(i * ROWS, INST, stride=VARS * ROWS)
                view[at, :] = view[at, :] + east_in[turn, i]

        @pl.when(has_next)
        def _():
            west.wait_recv()
            for i in range(VARS):
                at = pl.ds(i * ROWS + CX - 1, INST, stride=VARS * ROWS)
                view[at, :] = view[at, :] + west_in[turn, i]

    def couple(field):
        @pl.loop(0, INST // BLOCK)
        def _(n):
            at = pl.ds(n * BLOCK, BLOCK)
            state = [field[at, a] for a in range(VARS)]
            where_from = jnp.broadcast_to(partner[...][None], (BLOCK, ROWS, LANES))
            for i in range(VARS):
                terms = []
                for block in (EAST, WEST, PAIR):
                    total = blocks[block, 0, i][None] * state[0]
                    for a in range(1, VARS):
                        total = total + blocks[block, a, i][None] * state[a]
                    terms.append(total)
                east = jnp.where(row == 0, 0.0, pltpu.roll(terms[0], 1, 1))
                west = jnp.where(row == CX - 1, 0.0, pltpu.roll(terms[1], ROWS - 1, 1))
                pair = jnp.take_along_axis(terms[2], where_from, axis=1, mode="promise_in_bounds")
                offdiag[at, i] = east + west + pair

        weights = time_weights()

        @pl.loop(0, VARS)
        def _(i):
            offdiag[:, i] = offdiag[:, i] + scale[...][None] * cyclic(weights, field[:, i])

    def solve(n, to):
        at = pl.ds(n * BLOCK, BLOCK)
        rest = [source[at, a] - offdiag[at, a] for a in range(VARS)]
        for i in range(VARS):
            total = blocks[INV, 0, i][None] * rest[0]
            for a in range(1, VARS):
                total = total + blocks[INV, a, i][None] * rest[a]
            to[at, i] = total

    own[6].wait()
    for copy in gathers[0]:
        copy.wait_recv()
    send_halo(0, first)
    couple(first)
    take_halo(0)
    own[7].wait()
    for copy in gathers[1]:
        copy.wait_recv()

    @pl.loop(0, INST // BLOCK)
    def _(n):
        solve(n, second)

    send_halo(1, second)
    couple(second)
    take_halo(1)

    def back(peer):
        return pltpu.make_async_remote_copy(
            src_ref=result.at[pl.ds(peer * OWN, OWN), :, cells, :],
            dst_ref=out_hbm.at[:, :, :, columns(tm)],
            send_sem=back_send.at[peer],
            recv_sem=back_recv.at[tm],
            device_id=(peer, space),
            device_id_type=MESH,
        )

    own_back = pltpu.make_async_copy(
        result.at[pl.ds(tm * OWN, OWN), :, cells, :], out_hbm.at[:, :, :, columns(tm)], local_sem.at[0]
    )
    group = BLOCK // OWN

    @pl.loop(0, TM // group)
    def _(step):
        n = lax.rem(tm // group + step + 2, TM // group)
        solve(n, result)
        for k in range(group):
            peer = n * group + k

            @pl.when(peer != tm)
            def _():
                back(peer).start()

            @pl.when(peer == tm)
            def _():
                own_back.start()

    for copies in gathers:
        for copy in copies:
            copy.wait_send()
    for turn in range(2):
        east, west = halo_copies(turn)

        @pl.when(has_next)
        def _():
            east.wait_send()

        @pl.when(has_previous)
        def _():
            west.wait_send()

    own_back.wait()

    @pl.loop(0, TM)
    def _(peer):
        @pl.when(peer != tm)
        def _():
            back(peer).wait_send()
            pltpu.make_async_remote_copy(
                src_ref=result.at[pl.ds(0, OWN), :, cells, :],
                dst_ref=out_hbm.at[:, :, :, columns(peer)],
                send_sem=back_send.at[peer],
                recv_sem=back_recv.at[peer],
                device_id=(peer, space),
                device_id_type=MESH,
            ).wait_recv()


def local(
    adjoint_start, source, inv_diagonal, east_block, west_block, pair_block, time_scale, partner
):
    f32 = jnp.float32
    field = pltpu.VMEM((INST, VARS, ROWS, LANES), f32)
    halo = pltpu.VMEM((2, VARS, INST, LANES), f32)
    dma = pltpu.SemaphoreType.DMA
    return pl.pallas_call(
        kernel,
        out_shape=jax.ShapeDtypeStruct(adjoint_start.shape, f32),
        in_specs=[pl.BlockSpec(memory_space=pl.ANY)] * 8,
        out_specs=pl.BlockSpec(memory_space=pl.ANY),
        scratch_shapes=[
            field,
            field,
            field,
            field,
            field,
            pltpu.VMEM((4, VARS, VARS, CX, LANES), jnp.bfloat16),
            pltpu.VMEM((4, VARS, VARS, ROWS, LANES), f32),
            pltpu.VMEM((ROWS, LANES), f32),
            pltpu.VMEM((ROWS, LANES), jnp.int32),
            halo,
            halo,
            halo,
            halo,
            dma((8,)),
            dma((2, TM)),
            dma((2, TM)),
            dma((2, 2)),
            dma((2, 2)),
            dma((TM,)),
            dma((TM,)),
        ],
        compiler_params=pltpu.CompilerParams(
            collective_id=0, has_side_effects=True, vmem_limit_bytes=32 << 20
        ),
    )(adjoint_start, source, inv_diagonal, east_block, west_block, pair_block, time_scale, partner)


def solution(mesh):
    return jax.shard_map(
        local,
        mesh=mesh,
        in_specs=(
            P("tm", None, "space", None),
            P("tm", None, "space", None),
            P(None, None, "space", None),
            P(None, None, "space", None),
            P(None, None, "space", None),
            P(None, None, "space", None),
            P("space", None),
            P("space", None),
        ),
        out_specs=P("tm", None, "space", None),
        check_vma=False,
    )
```

time: 301 us -> 57.3 us (0.19)
  the two profiles are of different devices: /device:TPU:1 before, /device:TPU:14 now
where the time goes in v1:
time: 57.3 us; the launch traced here: 57.1 us
  Pallas kernels  51 us (89%)
  local copies, waits for them, and re-layouts  6 us (10%)
    pallas_call x1, Pallas kernels, local(): pl.pallas_call(kernel, out_shape=jax.ShapeDtypeStruct(adjoint_start.shape...  51 us
    unnamed x16, local copies, waits for them, and re-layouts  4.84 us
    pallas_call x1, local copies, waits for them, and re-layouts, local(): pl.pallas_call(kernel, out_shape=jax.ShapeDtypeStruct(adjoint_start.shape...  1.16 us

profile of v1, /device:TPU:14, one launch (start us, length us, event | category | flops | bytes accessed | tf_op | source)
XLA Modules:
  0.0 57.1 jit_solution(1448224880551019711)
XLA Ops:
  0.0 0.0 copy-start.6
  0.0 0.0 copy-start.1
  0.0 1.4 %copy.9.start_hbm = f32[2,5,6,2048]{3,2,1,0:T(8,128)S(1)} copy(f32[2,5,6,2048]{3,0,2,1:T(2,128)} %param.8) | data formatting | bytes 983040 | tf_op args[0]
  1.4 0.0 copy-done.6
  1.4 0.0 copy-start
  1.5 0.0 copy-start.4
  1.5 0.0 copy-start.5
  1.5 0.3 copy.10.source_hbm
  1.8 0.0 copy-done.1
  1.8 0.8 %copy-done = bf16[5,5,6,2048]{3,2,1,0:T(8,128)(2,1)S(1)} copy-done((bf16[5,5,6,2048]{3,2,1,0:T(8,128)(2,1)S(1)}, bf16[5,5,6,2048]{3,2,1,0:T(8,128)(2,1)}, u32[]{:S(2)}) %copy-start) | copy-done | bytes 614424
  2.6 0.0 copy-done.4
  2.6 0.0 copy-done.5
  2.6 0.0 copy-start.2
  2.6 1.1 %copy-done.2 = bf16[5,5,6,2048]{3,2,1,0:T(8,128)(2,1)S(1)} copy-done((bf16[5,5,6,2048]{3,2,1,0:T(8,128)(2,1)S(1)}, bf16[5,5,6,2048]{3,2,1,0:T(8,128)(2,1)}, u32[]{:S(2)}) %copy-start.2) | copy-done | bytes 614424
  3.7 0.0 copy-start.3
  3.8 1.1 %copy-done.3 = bf16[5,5,6,2048]{3,2,1,0:T(8,128)(2,1)S(1)} copy-done((bf16[5,5,6,2048]{3,2,1,0:T(8,128)(2,1)S(1)}, bf16[5,5,6,2048]{3,2,1,0:T(8,128)(2,1)}, u32[]{:S(2)}) %copy-start.3) | copy-done | bytes 614424
  4.9 51.0 %shard_map.82 = f32[2,5,6,2048]{3,2,1,0:T(8,128)S(1)} custom-call(f32[2,5,6,2048]{3,2,1,0:T(8,128)S(1)} %copy.9.start_hbm, f32[2,5,6,2048]{3,2,1,0:T(8,128)S(1)} %copy.10.source_hbm, bf16[5,5,6,2048]{3,2,1,0:T(8,128)(2,1)S(1)} %copy-done, bf16[5,5,6,2048]{3,2,1,0:T(8,128)(2,1)S(1)} %copy-done.1, bf16[5,5,6,2048]{3,2,1,0:T(8,128)(2,1)S(1)} %copy-done.2, ...), custom_call_target="tpu_custom_call" | custom-call | tf_op jit(solution)/shard_map/pallas_call | solution.py:337
  55.9 1.2 %copy.11 = f32[2,5,6,2048]{3,0,2,1:T(2,128)} copy(f32[2,5,6,2048]{3,2,1,0:T(8,128)S(1)} %shard_map.82) | data formatting | bytes 983040 | tf_op jit(solution)/shard_map/pallas_call | solution.py:337
Async XLA Ops:
  0.0 1.4 %copy-start.6 = (f32[2,5,6,2048]{3,0,2,1:T(2,128)S(1)}, f32[2,5,6,2048]{3,0,2,1:T(2,128)}, u32[]{:S(2)}) copy-start(f32[2,5,6,2048]{3,0,2,1:T(2,128)} %param.9) | copy-start | bytes 1474564
  0.0 1.8 %copy-start.1 = (bf16[5,5,6,2048]{3,2,1,0:T(8,128)(2,1)S(1)}, bf16[5,5,6,2048]{3,2,1,0:T(8,128)(2,1)}, u32[]{:S(2)}) copy-start(bf16[5,5,6,2048]{3,2,1,0:T(8,128)(2,1)} %east_hbm.1) | copy-start | bytes 1843204
  1.4 1.1 %copy-start = (bf16[5,5,6,2048]{3,2,1,0:T(8,128)(2,1)S(1)}, bf16[5,5,6,2048]{3,2,1,0:T(8,128)(2,1)}, u32[]{:S(2)}) copy-start(bf16[5,5,6,2048]{3,2,1,0:T(8,128)(2,1)} %inv_hbm.1) | copy-start | bytes 1843204
  1.5 1.1 %copy-start.4 = (f32[6,2048]{1,0:T(8,128)S(1)}, f32[6,2048]{1,0:T(8,128)}, u32[]{:S(2)}) copy-start(f32[6,2048]{1,0:T(8,128)} %scale_hbm.1) | copy-start | bytes 147460
  1.5 1.1 %copy-start.5 = (s32[6,2048]{1,0:T(8,128)S(1)}, s32[6,2048]{1,0:T(8,128)}, u32[]{:S(2)}) copy-start(s32[6,2048]{1,0:T(8,128)} %partner_hbm.1) | copy-start | bytes 147460
  2.6 1.1 %copy-start.2 = (bf16[5,5,6,2048]{3,2,1,0:T(8,128)(2,1)S(1)}, bf16[5,5,6,2048]{3,2,1,0:T(8,128)(2,1)}, u32[]{:S(2)}) copy-start(bf16[5,5,6,2048]{3,2,1,0:T(8,128)(2,1)} %west_hbm.1) | copy-start | bytes 1843204
  3.7 1.1 %copy-start.3 = (bf16[5,5,6,2048]{3,2,1,0:T(8,128)(2,1)S(1)}, bf16[5,5,6,2048]{3,2,1,0:T(8,128)(2,1)}, u32[]{:S(2)}) copy-start(bf16[5,5,6,2048]{3,2,1,0:T(8,128)(2,1)} %pair_hbm.1) | copy-start | bytes 1843204
